TPU v7x, 32 devices: a whole 2x2x4 slice. The times are simulated.
32 devices in a mesh: delay: 8 (over z, y), row: 2 (over core), col: 2 (over x).
Axes of the slice: x: 2, y: 2, z: 4, core: 2. Of those that a mesh axis runs over, the one named last changes fastest.
Arguments:
- delays: float32 [8, 4096, 2, 2048], P('delay', 'row', None, 'col'), may hold values from -0.015625 to 0.015625
- history: float32 [8, 256, 4096], P('delay', None, ('row', 'col')), may hold values from -6 to 6
- sources: float32 [4, 256, 4096], P(None, None, ('row', 'col')), may hold values from -6 to 6
- self_inverse: float32 [16, 256, 256], P(('row', 'col')), may hold values from -4 to 4, as said below
Outputs:
- adjoints: float32 [4, 256, 4096], P(None, None, ('row', 'col'))
Inputs may be any that keep to these rules, and one draw needn't show every extreme that they name: `self_inverse`: dense blocks.
All inputs are finite; a program needn't handle non-finite values.
Results may differ from a plain program's by a relative error of at most 0.0001.
Values sent between devices are 32-bit elements; how exact they have to be, the bound alone decides.
A program may use at most 128 MiB of HBM per device.

v0:
```python
import jax
import jax.numpy as jnp
from jax import lax
from jax.sharding import PartitionSpec as P


def from_behind(shard, axis, by):
    devices = lax.axis_size(axis)
    pairs = [(i, i + by) for i in range(devices) if 0 <= i + by < devices]
    return lax.ppermute(shard, axis, pairs)


def apply_blocks(drive, self_inverse):
    count = drive.shape[0]
    blocks = self_inverse.shape[0]
    order = self_inverse.shape[1]
    shaped = drive.reshape(count, blocks, order)
    result = jnp.einsum("rbs,bst->rbt", shaped, self_inverse, precision=lax.Precision.HIGHEST)
    return result.reshape(count, blocks * order)


def partial_products(hist, tiles):
    wide = lax.all_gather(hist, "row", axis=2, tiled=True)

    def terms(start, size):
        return jnp.einsum("krj,kij->ri", wide, tiles, precision=lax.Precision.HIGHEST)

    return terms


def on_device(delays, history, sources, self_inverse):
    local_count = delays.shape[0]
    out_rows = delays.shape[1]
    tiles = delays.reshape(local_count, out_rows, -1)
    excite = history.shape[1]
    count = sources.shape[0]
    hist = history
    results = []
    for step in range(count):
        terms = partial_products(hist, tiles)
        summed = lax.psum_scatter(terms(0, excite), "col", scatter_dimension=1, tiled=True)
        coupled = lax.psum(summed, "delay")
        adjoint = apply_blocks(sources[step] - coupled, self_inverse)
        results.append(adjoint)
        if step + 1 < count:
            carried = from_behind(hist[local_count - 1], "delay", 1)
            head = jnp.where(lax.axis_index("delay") == 0, adjoint, carried)
            hist = jnp.concatenate([head[None], hist[: local_count - 1]], axis=0)
    return jnp.stack(results, axis=0)


def solution(mesh):
    placed = (
        P("delay", "row", None, "col"),
        P("delay", None, ("row", "col")),
        P(None, None, ("row", "col")),
        P(("row", "col"), None, None),
    )
    return jax.shard_map(
        on_device,
        mesh=mesh,
        in_specs=placed,
        out_specs=P(None, None, ("row", "col")),
        check_vma=False,
    )
```

profile of v0, /device:TPU:28, one launch (start us, length us, event | category | flops | bytes accessed | tf_op | source)
XLA Modules:
  0.0 652.0 jit_solution(2965975356141721326)
XLA Ops:
  7.3 15.7 %copy.28 = f32[256,8,2,1024]{3,1,2,0:T(8,128)} copy(f32[256,8,2,1024]{3,2,1,0:T(2,128)} %bitcast.64) | data formatting | bytes 33554432
  23.0 18.5 %fusion = f32[256,2048]{1,0:T(8,128)} fusion(f32[2048,2048]{1,0:T(8,128)} %bitcast.60, f32[1,256,2048]{2,1,0:T(8,128)} %all-gather.8.cloned.1.call-done), kind=kOutput, calls=%fused_computation.1 | convolution fusion | flops 12884901888 | bytes 20971520 | tf_op jit(solution)/shard_map/krj,kij->ri/dot_general | solution.py:26
  41.6 32.9 %reduce-scatter.5.cloned.1.call-done = f32[256,1024]{1,0:T(8,128)} async-done(((f32[256,2048]{1,0:T(8,128)}), f32[256,1024]{1,0:T(8,128)}) %reduce-scatter.5.cloned.1.call-update) | async-done | bytes 1048592 | tf_op jit(solution)/shard_map/reduce_scatter | solution.py:41
  75.8 88.4 %all-reduce.5.cloned.1.call-done = f32[256,1024]{1,0:T(8,128)} async-done(((f32[256,1024]{1,0:T(8,128)}), f32[256,1024]{1,0:T(8,128)}) %all-reduce.5.cloned.1.call-update) | async-done | bytes 1048592 | tf_op jit(solution)/shard_map/psum | solution.py:42
  168.1 2.3 broadcast_select_fusion.2
  170.7 11.7 %all-gather.10.cloned.1.call-done = f32[256,2048]{1,0:T(8,128)} async-done(((f32[256,1024]{1,0:T(8,128)}), f32[256,2048]{1,0:T(8,128)}) %all-gather.10.cloned.1.call-update) | async-done | bytes 2097168 | tf_op jit(solution)/shard_map/all_gather | solution.py:23
  182.3 18.5 %fusion.14 = f32[256,2048]{1,0:T(8,128)} fusion(f32[256,2048]{1,0:T(8,128)} %all-gather.10.cloned.1.call-done, f32[2048,2048]{1,0:T(8,128)} %bitcast.61), kind=kOutput, calls=%fused_computation.22 | convolution fusion | flops 12884901888 | bytes 20971520 | tf_op jit(solution)/shard_map/krj,kij->ri/dot_general | solution.py:26
  200.9 32.9 %reduce-scatter.7.cloned.1.call-done = f32[256,1024]{1,0:T(8,128)} async-done(((f32[256,2048]{1,0:T(8,128)}), f32[256,1024]{1,0:T(8,128)}) %reduce-scatter.7.cloned.1.call-update) | async-done | bytes 1048592 | tf_op jit(solution)/shard_map/reduce_scatter | solution.py:41
  235.1 88.2 %all-reduce.7.cloned.1.call-done = f32[256,1024]{1,0:T(8,128)} async-done(((f32[256,1024]{1,0:T(8,128)}), f32[256,1024]{1,0:T(8,128)}) %all-reduce.7.cloned.1.call-update) | async-done | bytes 1048592 | tf_op jit(solution)/shard_map/psum | solution.py:42
  325.0 1.9 fusion.8
  328.1 2.4 broadcast_select_fusion.1
  330.6 11.9 %all-gather.12.cloned.1.call-done = f32[256,2048]{1,0:T(8,128)} async-done(((f32[256,1024]{1,0:T(8,128)}), f32[256,2048]{1,0:T(8,128)}) %all-gather.12.cloned.1.call-update) | async-done | bytes 2097168 | tf_op jit(solution)/shard_map/all_gather | solution.py:23
  342.5 18.5 %fusion.15 = f32[256,2048]{1,0:T(8,128)} fusion(f32[256,2048]{1,0:T(8,128)} %all-gather.12.cloned.1.call-done, f32[2048,2048]{1,0:T(8,128)} %bitcast.62), kind=kOutput, calls=%fused_computation.23 | convolution fusion | flops 12884901888 | bytes 20971520 | tf_op jit(solution)/shard_map/krj,kij->ri/dot_general | solution.py:26
  361.0 32.9 %reduce-scatter.9.cloned.1.call-done = f32[256,1024]{1,0:T(8,128)} async-done(((f32[256,2048]{1,0:T(8,128)}), f32[256,1024]{1,0:T(8,128)}) %reduce-scatter.9.cloned.1.call-update) | async-done | bytes 1048592 | tf_op jit(solution)/shard_map/reduce_scatter | solution.py:41
  395.5 88.1 %all-reduce.9.cloned.1.call-done = f32[256,1024]{1,0:T(8,128)} async-done(((f32[256,1024]{1,0:T(8,128)}), f32[256,1024]{1,0:T(8,128)}) %all-reduce.9.cloned.1.call-update) | async-done | bytes 1048592 | tf_op jit(solution)/shard_map/psum | solution.py:42
  485.3 2.8 fusion.5
  488.1 2.5 copy.13
  490.6 2.4 broadcast_select_fusion
  493.1 11.9 %all-gather.14.cloned.1.call-done = f32[256,2048]{1,0:T(8,128)} async-done(((f32[256,1024]{1,0:T(8,128)}), f32[256,2048]{1,0:T(8,128)}) %all-gather.14.cloned.1.call-update) | async-done | bytes 2097168 | tf_op jit(solution)/shard_map/all_gather | solution.py:23
  504.9 18.5 %fusion.16 = f32[256,2048]{1,0:T(8,128)} fusion(f32[256,2048]{1,0:T(8,128)} %all-gather.14.cloned.1.call-done, f32[2048,2048]{1,0:T(8,128)} %bitcast.63), kind=kOutput, calls=%fused_computation.24 | convolution fusion | flops 12884901888 | bytes 20971520 | tf_op jit(solution)/shard_map/krj,kij->ri/dot_general | solution.py:26
  523.5 32.9 %reduce-scatter.11.cloned.1.call-done = f32[256,1024]{1,0:T(8,128)} async-done(((f32[256,2048]{1,0:T(8,128)}), f32[256,1024]{1,0:T(8,128)}) %reduce-scatter.11.cloned.1.call-update) | async-done | bytes 1048592 | tf_op jit(solution)/shard_map/reduce_scatter | solution.py:41
  559.0 2.5 copy.18
  561.6 75.3 %all-reduce.11.cloned.1.call-done = f32[256,1024]{1,0:T(8,128)} async-done(((f32[256,1024]{1,0:T(8,128)}), f32[256,1024]{1,0:T(8,128)}) %all-reduce.11.cloned.1.call-update) | async-done | bytes 1048592 | tf_op jit(solution)/shard_map/psum | solution.py:42
  640.7 4.5 pad_maximum_fusion
  (44 shorter events, 20.7 us)
Async XLA Ops:
  6.5 159.3 %copy-start = (f32[4,256,256]{2,1,0:T(8,128)S(1)}, f32[4,256,256]{2,1,0:T(8,128)}, u32[]{:S(2)}) copy-start(f32[4,256,256]{2,1,0:T(8,128)} %param.7) | copy-start | bytes 3145732
  6.5 16.5 %all-gather.8.cloned.1.call-start = ((), (), s32[]{:S(2)}) async-start(), calls=%async_computation.4 | async-start | bytes 3145728 | tf_op jit(solution)/shard_map/all_gather | solution.py:23
  7.3 67.2 %reduce-scatter.5.cloned.1.call-start = ((), (), s32[]{:S(2)}) async-start(), calls=%async_computation.5 | async-start | bytes 3145728 | tf_op jit(solution)/shard_map/reduce_scatter | solution.py:41
  41.5 122.6 %all-reduce.5.cloned.1.call-start = ((), (), s32[]{:S(2)}) async-start(), calls=%async_computation.6 | async-start | bytes 2097152 | tf_op jit(solution)/shard_map/psum | solution.py:42
  74.4 107.9 %all-gather.10.cloned.1.call-start = ((), (), s32[]{:S(2)}) async-start(), calls=%async_computation.13 | async-start | bytes 3145728 | tf_op jit(solution)/shard_map/all_gather | solution.py:23
  74.5 93.6 %collective-permute-start = (f32[256,1024]{1,0:T(8,128)}, f32[256,1024]{1,0:T(8,128)}, u32[]{:S(2)}, u32[]{:S(2)}) collective-permute-start(f32[256,1024]{1,0:T(8,128)} %bitcast.6), channel_id=1, source_target_pairs={{0,4},{4,8},{8,12},{12,16},{16,20},{20,24},{24,28},{1,5},{5,9},{9,... | collective-permute-start | bytes 3145736 | tf_op jit(solution)/shard_map/ppermute | solution.py:10
  170.4 63.3 %reduce-scatter.7.cloned.1.call-start = ((), (), s32[]{:S(2)}) async-start(), calls=%async_computation.7 | async-start | bytes 3145728 | tf_op jit(solution)/shard_map/reduce_scatter | solution.py:41
  200.8 122.5 %all-reduce.7.cloned.1.call-start = ((), (), s32[]{:S(2)}) async-start(), calls=%async_computation.8 | async-start | bytes 2097152 | tf_op jit(solution)/shard_map/psum | solution.py:42
  233.7 108.8 %all-gather.12.cloned.1.call-start = ((), (), s32[]{:S(2)}) async-start(), calls=%async_computation.14 | async-start | bytes 3145728 | tf_op jit(solution)/shard_map/all_gather | solution.py:23
  233.8 94.4 %collective-permute-start.1 = (f32[256,1024]{1,0:T(8,128)}, f32[256,1024]{1,0:T(8,128)}, u32[]{:S(2)}, u32[]{:S(2)}) collective-permute-start(f32[256,1024]{1,0:T(8,128)} %broadcast_select_fusion.2), channel_id=1, source_target_pairs={{0,4},{4,8},{8,12},{12,16},{16,20},{20,24},{24,28},{1,5},{5,9},{9,... | collective-permute-start | bytes 3145736 | tf_op jit(solution)/shard_map/ppermute | solution.py:10
  330.6 63.3 %reduce-scatter.9.cloned.1.call-start = ((), (), s32[]{:S(2)}) async-start(), calls=%async_computation.9 | async-start | bytes 3145728 | tf_op jit(solution)/shard_map/reduce_scatter | solution.py:41
  361.0 122.6 %all-reduce.9.cloned.1.call-start = ((), (), s32[]{:S(2)}) async-start(), calls=%async_computation.10 | async-start | bytes 2097152 | tf_op jit(solution)/shard_map/psum | solution.py:42
  393.9 111.0 %all-gather.14.cloned.1.call-start = ((), (), s32[]{:S(2)}) async-start(), calls=%async_computation.15 | async-start | bytes 3145728 | tf_op jit(solution)/shard_map/all_gather | solution.py:23
  394.0 96.7 %collective-permute-start.2 = (f32[256,1024]{1,0:T(8,128)}, f32[256,1024]{1,0:T(8,128)}, u32[]{:S(2)}, u32[]{:S(2)}) collective-permute-start(f32[256,1024]{1,0:T(8,128)} %broadcast_select_fusion.1), channel_id=1, source_target_pairs={{0,4},{4,8},{8,12},{12,16},{16,20},{20,24},{24,28},{1,5},{5,9},{9,... | collective-permute-start | bytes 3145736 | tf_op jit(solution)/shard_map/ppermute | solution.py:10
  493.0 63.3 %reduce-scatter.11.cloned.1.call-start = ((), (), s32[]{:S(2)}) async-start(), calls=%async_computation.11 | async-start | bytes 3145728 | tf_op jit(solution)/shard_map/reduce_scatter | solution.py:41
  523.4 113.4 %all-reduce.11.cloned.1.call-start = ((), (), s32[]{:S(2)}) async-start(), calls=%async_computation.12 | async-start | bytes 2097152 | tf_op jit(solution)/shard_map/psum | solution.py:42
Sparse Core Ops, SparseCore 0:
  8.9 11.7 all-gather.7
  41.6 32.7 reduce-scatter.4
  78.3 85.7 all-reduce.4
  170.5 11.7 all-gather.9
  200.9 32.7 reduce-scatter.6
  237.5 85.7 all-reduce.6
  330.7 11.7 all-gather.11
  361.1 32.7 reduce-scatter.8
  397.8 85.7 all-reduce.8
  493.2 11.7 all-gather.13
  523.6 32.7 reduce-scatter.10
  560.1 76.6 all-reduce.10
where the time goes:
time: 656 us; the launch traced here: 652 us
  waiting for transfers between devices  508 us (77%)
  matrix products  82.2 us (13%)
  local copies, waits for them, and re-layouts  25.4 us (4%)
  other arithmetic  18.4 us (3%)
  between operations  13.7 us (2%)
    psum x4, waiting for transfers between devices, on_device(): coupled = lax.psum(summed, 'delay')  340 us
    reduce_scatter x4, waiting for transfers between devices, on_device(): lax.psum_scatter(terms(0, excite), 'col', scatter_dimension=1, tiled=True)  131 us
    dot_general x4, matrix products, terms(): jnp.einsum('krj,kij->ri', wide, tiles, precision=lax.Precision.HIGHEST)  73.8 us
    all_gather x4, waiting for transfers between devices, partial_products(): wide = lax.all_gather(hist, 'row', axis=2, tiled=True)  35.4 us
    unnamed x3, local copies, waits for them, and re-layouts  15.7 us
  transfers between devices with their start and end apart: 15, of which 11 were waited for; matrix products, arithmetic and copies ran while one was open for 6% of the time, Pallas kernels for 0%

commit v1 on v0

v1 whole, which is shorter than its diff:
```python
import functools

import jax
import jax.numpy as jnp
from jax import lax
from jax.experimental import pallas as pl
from jax.experimental.pallas import tpu as pltpu
from jax.sharding import PartitionSpec as P

MESH = pl.DeviceIdType.MESH
GROUPS = 2


def split_two(x):
    high = x.astype(jnp.bfloat16)
    low = (x - high.astype(jnp.float32)).astype(jnp.bfloat16)
    return high, low


def times_transposed(a, b):
    return lax.dot_general(a, b, (((1,), (1,)), ((), ())), preferred_element_type=jnp.float32)


def kernel(
    sizes, m_high, m_low, hist, sources, inverse, out,
    xs, partner, older, p_send, p_recv, total, z_recv, y_recv,
    x_send_sem, x_recv_sem, z_send_sem, z_recv_sem, y_recv_sem,
    b_one_sem, b_two_sem, b_recv_sem, r_send_sem, r_recv_sem, h_send_sem, h_recv_sem,
):
    n_delay, n_col, steps, rows, blocks, order = sizes
    items = steps * GROUPS
    part = rows // GROUPS
    width = blocks * order
    k = lax.axis_index("delay")
    r = lax.axis_index("row")
    c = lax.axis_index("col")
    has_one = k + 1 < n_delay
    has_two = k + 2 < n_delay

    def remote(src, dst, send, recv, **where):
        return pltpu.make_async_remote_copy(
            src_ref=src, dst_ref=dst, send_sem=send, recv_sem=recv,
            device_id=where, device_id_type=MESH,
        )

    def arrived(ref, sem):
        remote(ref, ref, sem, sem, row=1 - r).wait_recv()

    def col_at(by):
        return lax.rem(c + by, n_col)

    barrier = pltpu.get_barrier_semaphore()

    def greet(**where):
        pl.semaphore_signal(barrier, inc=1, device_id=where, device_id_type=MESH)

    greet(row=1 - r)
    for by in range(1, n_col):
        greet(col=col_at(by))
    pl.when(has_one)(lambda: greet(delay=k + 1))
    pl.when(has_two)(lambda: greet(delay=k + 2))
    pl.when(k >= 1)(lambda: greet(delay=k - 1))
    pl.when(k >= 2)(lambda: greet(delay=k - 2))
    peers = n_col
    for there in (has_one, has_two, k >= 1, k >= 2):
        peers = peers + jnp.where(there, 1, 0)
    pl.semaphore_wait(barrier, peers)

    def rows_of(g):
        return pl.ds(pl.multiple_of(g * part, part), part)

    def cell(s, g, b):
        return out.at[s, rows_of(g), pl.ds(pl.multiple_of(b * order, order), order)]

    def older_copy(src, j, g, by):
        return remote(src, older.at[j, rows_of(g)], h_send_sem.at[j, g], h_recv_sem.at[j, g], delay=k + by)

    def put(half, value):
        high, low = split_two(value)
        xs[half, pl.ds(0, part)] = high
        xs[half, pl.ds(part, part)] = low

    def to_partner(src, n):
        return remote(src, partner.at[n], r_send_sem.at[n], r_recv_sem.at[n], row=1 - r)

    def tile(first):
        at = pl.ds(pl.multiple_of(first, order), order)
        acc = jnp.zeros((part, order), jnp.float32)
        for h in range(2):
            high = m_high[at, h * width:(h + 1) * width]
            low = m_low[at, h * width:(h + 1) * width]
            both = times_transposed(xs[h], high)
            acc = acc + (both[:part] + both[part:] + times_transposed(xs[h, :part], low))
        return acc

    def p_copy(n, by, b):
        return remote(
            p_send.at[n, by - 1, b], p_recv.at[n, by - 1, b],
            x_send_sem.at[n, by - 1], x_recv_sem.at[n, by - 1, b], col=col_at(by),
        )

    def multiply(n):
        s, g = n // GROUPS, n % GROUPS

        @pl.when(s == 0)
        def _():
            to_partner(hist.at[rows_of(g)], n).start()
            pl.when(has_one)(lambda: older_copy(hist.at[rows_of(g)], 0, g, 1).start())
            put(r, hist[rows_of(g)])

        @pl.when((s >= 1) & (k >= s))
        def _():
            arrived(older.at[s - 1, rows_of(g)], h_recv_sem.at[s - 1, g])
            to_partner(older.at[s - 1, rows_of(g)], n).start()
            if steps > 3:
                @pl.when((s == 1) & has_two)
                def _():
                    older_copy(older.at[0, rows_of(g)], 2, g, 2).start()
            put(r, older[s - 1, rows_of(g)])

        @pl.when((s >= 1) & (k < s))
        def _():
            to_partner(out.at[s - 1 - k, rows_of(g)], n).start()
            put(r, out[s - 1 - k, rows_of(g)])

        arrived(partner.at[n], r_recv_sem.at[n])
        put(1 - r, partner[n])

        for by in range(1, n_col):
            def far(b, carry):
                p_send[n, by - 1, b] = tile((col_at(by) * blocks + b) * order)
                p_copy(n, by, b).start()
                return carry

            lax.fori_loop(0, blocks, far, 0)

        def near(b, carry):
            total[n, b] = tile((c * blocks + b) * order)
            return carry

        lax.fori_loop(0, blocks, near, 0)

        @pl.when((s == 0) & has_two)
        def _():
            older_copy(hist.at[rows_of(g)], 1, g, 2).start()

    def z_copy(n, b):
        return remote(total.at[n, b], z_recv.at[n, b], z_send_sem.at[n], z_recv_sem.at[n, b], delay=k - 2)

    def y_copy(n, b):
        return remote(total.at[n, b], y_recv.at[n, b], z_send_sem.at[n], y_recv_sem.at[n, b], delay=k - 1)

    def b_copy(n, b, by, sem):
        s, g = n // GROUPS, n % GROUPS
        return remote(cell(s, g, b), cell(s, g, b), sem.at[n], b_recv_sem.at[n, b], delay=k + by)

    def reduce(n):
        s, g = n // GROUPS, n % GROUPS

        def one(b, carry):
            value = total[n, b]
            for by in range(1, n_col):
                arrived(p_recv.at[n, by - 1, b], x_recv_sem.at[n, by - 1, b])
                value = value + p_recv[n, by - 1, b]
            total[n, b] = value

            @pl.when(has_two)
            def _():
                arrived(z_recv.at[n, b], z_recv_sem.at[n, b])
                total[n, b] = total[n, b] + z_recv[n, b]

            pl.when(k >= 2)(lambda: z_copy(n, b).start())
            pl.when(k == 1)(lambda: y_copy(n, b).start())

            @pl.when(k == 0)
            def _():
                arrived(y_recv.at[n, b], y_recv_sem.at[n, b])
                at = pl.ds(pl.multiple_of(b * order, order), order)
                drive = sources[s, rows_of(g), at] - (total[n, b] + y_recv[n, b])
                out[s, rows_of(g), at] = jnp.dot(
                    drive, inverse[b], precision=lax.Precision.HIGHEST,
                    preferred_element_type=jnp.float32,
                )
                b_copy(n, b, 1, b_one_sem).start()
                if n_delay > 2:
                    b_copy(n, b, 2, b_two_sem).start()

            return carry

        lax.fori_loop(0, blocks, one, 0)

    def pass_on(n):
        s, g = n // GROUPS, n % GROUPS

        def one(b, carry):
            arrived(cell(s, g, b), b_recv_sem.at[n, b])
            pl.when(has_two)(lambda: b_copy(n, b, 2, b_two_sem).start())
            return carry

        @pl.when(k >= 1)
        def _():
            lax.fori_loop(0, blocks, one, 0)

    def turn(i, carry):
        pl.when((i >= GROUPS) & (i < items + GROUPS))(lambda: reduce(i - GROUPS))
        pl.when(i >= 2 * GROUPS)(lambda: pass_on(i - 2 * GROUPS))
        pl.when(i < items)(lambda: multiply(i))
        return carry

    lax.fori_loop(0, items + 2 * GROUPS, turn, 0)

    def whole_send(ref, sem):
        remote(ref, ref, sem, sem, row=1 - r).wait_send()

    def settle(n, carry):
        s, g = n // GROUPS, n % GROUPS
        for by in range(1, n_col):
            whole_send(p_send.at[n, by - 1], x_send_sem.at[n, by - 1])
        whole_send(partner.at[n], r_send_sem.at[n])
        pl.when(k >= 1)(lambda: whole_send(total.at[n], z_send_sem.at[n]))
        pl.when(k == 0)(lambda: whole_send(out.at[s, rows_of(g)], b_one_sem.at[n]))
        pl.when(has_two)(lambda: whole_send(out.at[s, rows_of(g)], b_two_sem.at[n]))
        return carry

    lax.fori_loop(0, items, settle, 0)
    for g in range(GROUPS):
        pl.when(has_one)(lambda: whole_send(partner.at[0], h_send_sem.at[0, g]))
        pl.when(has_two)(lambda: whole_send(partner.at[0], h_send_sem.at[1, g]))
        pl.when((k >= 1) & has_two)(lambda: whole_send(partner.at[0], h_send_sem.at[2, g]))


def on_device(n_delay, n_col, delays, history, sources, self_inverse):
    out_rows = delays.shape[1]
    tiles = delays.reshape(out_rows, -1)
    rounded = lax.reduce_precision(tiles, 8, 7)
    m_high = rounded.astype(jnp.bfloat16)
    m_low = (tiles - rounded).astype(jnp.bfloat16)
    steps, rows, width = sources.shape
    blocks, order, _ = self_inverse.shape
    items, part = steps * GROUPS, rows // GROUPS
    sizes = (n_delay, n_col, steps, rows, blocks, order)
    dma = pltpu.SemaphoreType.DMA
    f32 = jnp.float32
    far = n_col - 1
    cells = (items, blocks, part, order)
    return pl.pallas_call(
        functools.partial(kernel, sizes),
        out_shape=jax.ShapeDtypeStruct(sources.shape, f32),
        in_specs=[pl.BlockSpec(memory_space=pltpu.VMEM)] * 5,
        out_specs=pl.BlockSpec(memory_space=pltpu.VMEM),
        scratch_shapes=[
            pltpu.VMEM((2, 2 * part, width), jnp.bfloat16),
            pltpu.VMEM((items, part, width), f32),
            pltpu.VMEM((steps - 1, rows, width), f32),
            pltpu.VMEM((items, far, blocks, part, order), f32),
            pltpu.VMEM((items, far, blocks, part, order), f32),
            pltpu.VMEM(cells, f32),
            pltpu.VMEM(cells, f32),
            pltpu.VMEM(cells, f32),
            dma((items, far)),
            dma((items, far, blocks)),
            dma((items,)),
            dma((items, blocks)),
            dma((items, blocks)),
            dma((items,)),
            dma((items,)),
            dma((items, blocks)),
            dma((items,)),
            dma((items,)),
            dma((steps - 1, GROUPS)),
            dma((steps - 1, GROUPS)),
        ],
        compiler_params=pltpu.CompilerParams(
            collective_id=0, has_side_effects=True, vmem_limit_bytes=60 * 2**20
        ),
        cost_estimate=pl.CostEstimate(
            flops=6 * steps * rows * out_rows * tiles.shape[1], bytes_accessed=24 * 2**20, transcendentals=0
        ),
    )(m_high, m_low, history[0], sources, self_inverse)


def solution(mesh):
    placed = (
        P("delay", "row", None, "col"),
        P("delay", None, ("row", "col")),
        P(None, None, ("row", "col")),
        P(("row", "col"), None, None),
    )
    return jax.shard_map(
        functools.partial(on_device, mesh.shape["delay"], mesh.shape["col"]),
        mesh=mesh,
        in_specs=placed,
        out_specs=P(None, None, ("row", "col")),
        check_vma=False,
    )
```

time: 656 us -> 397 us (0.61)
  waiting for transfers between devices: 508 us -> 0 us
  Pallas kernels: 0 us -> 374 us
  matrix products: 82.2 us -> 0 us
  between operations: 13.7 us -> 0.02 us
  other arithmetic: 18.4 us -> 6.98 us
  local copies, waits for them, and re-layouts: 25.4 us -> 15.8 us
    pallas_call x0 -> x1, Pallas kernels: none -> 374 us  [on_device(): pl.pallas_call(functools.partial(kernel, sizes), out_shape=jax.ShapeDtype...]
    psum x4 -> x0, waiting for transfers between devices: 340 us -> none  [on_device(): coupled = lax.psum(summed, 'delay')]
    reduce_scatter x4 -> x0, waiting for transfers between devices: 131 us -> none  [on_device(): lax.psum_scatter(terms(0, excite), 'col', scatter_dimension=1, tiled=True)]
    dot_general x8 -> x0, matrix products: 82.2 us -> none  [the longest x4 73.8 us: terms(): jnp.einsum('krj,kij->ri', wide, tiles, precision=lax.Precision.HIGHEST)]
    all_gather x4 -> x0, waiting for transfers between devices: 35.4 us -> none  [partial_products(): wide = lax.all_gather(hist, 'row', axis=2, tiled=True)]
    select_n x3 -> x0, other arithmetic: 7.16 us -> none  [on_device(): head = jnp.where(lax.axis_index('delay') == 0, adjoint, carried)]
    convert_element_type x0 -> x1, other arithmetic: none -> 6.98 us  [on_device(): m_low = (tiles - rounded).astype(jnp.bfloat16)]
    sub x4 -> x0, other arithmetic: 6.75 us -> none  [on_device(): adjoint = apply_blocks(sources[step] - coupled, self_inverse)]
  transfers between devices with their start and end apart: 15 -> 0, of which waited for: 11 -> 0; matrix products, arithmetic and copies ran while one was open for 6% -> 0% of each run, Pallas kernels for 0% -> 0%
where the time goes in v1:
time: 397 us
  Pallas kernels  374 us (94%)
  local copies, waits for them, and re-layouts  15.8 us (4%)
  other arithmetic  6.98 us (2%)
    pallas_call x1, Pallas kernels, on_device(): pl.pallas_call(functools.partial(kernel, sizes), out_shape=jax.ShapeDtype...  374 us
    unnamed x2, local copies, waits for them, and re-layouts  15.8 us

profile of v1, /device:TPU:28, one launch (start us, length us, event | category | flops | bytes accessed | tf_op | source)
XLA Modules:
  0.0 397.1 jit_solution(15094332985533751969)
XLA Ops:
  0.0 11.0 %copy.5 = f32[256,8,2,1024]{3,1,2,0:T(8,128)S(1)} copy(f32[256,8,2,1024]{3,2,1,0:T(2,128)} %bitcast.5) | data formatting | bytes 33554432
  11.0 7.0 %fusion = (bf16[2048,2048]{1,0:T(8,128)(2,1)}, bf16[2048,2048]{1,0:T(8,128)(2,1)}) fusion(f32[2048,2048]{1,0:T(8,128)S(1)} %bitcast.4), kind=kLoop, calls=%fused_computation.2 | loop fusion | flops 16777216 | bytes 33554432 | tf_op jit(solution)/shard_map/convert_element_type | solution.py:237
  18.0 374.3 %shard_map.46 = f32[4,256,1024]{2,1,0:T(8,128)} custom-call(bf16[2048,2048]{1,0:T(8,128)(2,1)} %get-tuple-element.6.m_high, bf16[2048,2048]{1,0:T(8,128)(2,1)} %get-tuple-element.5.m_low, f32[256,1024]{1,0:T(8,128)} %bitcast.6, f32[4,256,1024]{2,1,0:T(8,128)} %sources.1, f32[4,256,256]{2,1,0:T(8,128)} %inverse.1), custom_call_target="tpu_custom_call" | custom-call | flops 25769803776 | bytes 25165824 | tf_op jit(solution)/shard_map/pallas_call | solution.py:246
  392.3 4.8 %copy.7 = f32[4,256,1024]{2,1,0:T(8,128)} copy(f32[4,256,1024]{2,1,0:T(8,128)} %shard_map.46) | data formatting | bytes 8388608

commit v2 on v1

--- a/solution.py
+++ b/solution.py
@@ -17,12 +17,12 @@
     return high, low
 
 
-def times_transposed(a, b):
-    return lax.dot_general(a, b, (((1,), (1,)), ((), ())), preferred_element_type=jnp.float32)
+def times(a, b):
+    return jnp.dot(a, b, preferred_element_type=jnp.float32)
 
 
 def kernel(
-    sizes, m_high, m_low, hist, sources, inverse, out,
+    sizes, high_0, high_1, low_0, low_1, hist, sources, inverse, out,
     xs, partner, older, p_send, p_recv, total, z_recv, y_recv,
     x_send_sem, x_recv_sem, z_send_sem, z_recv_sem, y_recv_sem,
     b_one_sem, b_two_sem, b_recv_sem, r_send_sem, r_recv_sem, h_send_sem, h_recv_sem,
@@ -76,21 +76,19 @@
         return remote(src, older.at[j, rows_of(g)], h_send_sem.at[j, g], h_recv_sem.at[j, g], delay=k + by)
 
     def put(half, value):
-        high, low = split_two(value)
-        xs[half, pl.ds(0, part)] = high
-        xs[half, pl.ds(part, part)] = low
+        high, low = split_two(value.T)
+        xs[half, :, :part] = high
+        xs[half, :, part:] = low
 
     def to_partner(src, n):
         return remote(src, partner.at[n], r_send_sem.at[n], r_recv_sem.at[n], row=1 - r)
 
     def tile(first):
         at = pl.ds(pl.multiple_of(first, order), order)
-        acc = jnp.zeros((part, order), jnp.float32)
-        for h in range(2):
-            high = m_high[at, h * width:(h + 1) * width]
-            low = m_low[at, h * width:(h + 1) * width]
-            both = times_transposed(xs[h], high)
-            acc = acc + (both[:part] + both[part:] + times_transposed(xs[h, :part], low))
+        acc = jnp.zeros((order, part), jnp.float32)
+        for h, (m_high, m_low) in enumerate(((high_0, low_0), (high_1, low_1))):
+            both = times(m_high[at], xs[h])
+            acc = acc + (both[:, :part] + both[:, part:] + times(m_low[at], xs[h, :, :part]))
         return acc
 
     def p_copy(n, by, b):
@@ -176,7 +174,7 @@
             def _():
                 arrived(y_recv.at[n, b], y_recv_sem.at[n, b])
                 at = pl.ds(pl.multiple_of(b * order, order), order)
-                drive = sources[s, rows_of(g), at] - (total[n, b] + y_recv[n, b])
+                drive = sources[s, rows_of(g), at] - (total[n, b] + y_recv[n, b]).T
                 out[s, rows_of(g), at] = jnp.dot(
                     drive, inverse[b], precision=lax.Precision.HIGHEST,
                     preferred_element_type=jnp.float32,
@@ -231,10 +229,10 @@
 
 def on_device(n_delay, n_col, delays, history, sources, self_inverse):
     out_rows = delays.shape[1]
-    tiles = delays.reshape(out_rows, -1)
-    rounded = lax.reduce_precision(tiles, 8, 7)
-    m_high = rounded.astype(jnp.bfloat16)
-    m_low = (tiles - rounded).astype(jnp.bfloat16)
+    halves = [delays[0, :, h, :] for h in range(2)]
+    rounded = [lax.reduce_precision(half, 8, 7) for half in halves]
+    highs = [x.astype(jnp.bfloat16) for x in rounded]
+    lows = [(half - x).astype(jnp.bfloat16) for half, x in zip(halves, rounded)]
     steps, rows, width = sources.shape
     blocks, order, _ = self_inverse.shape
     items, part = steps * GROUPS, rows // GROUPS
@@ -242,18 +240,18 @@
     dma = pltpu.SemaphoreType.DMA
     f32 = jnp.float32
     far = n_col - 1
-    cells = (items, blocks, part, order)
+    cells = (items, blocks, order, part)
     return pl.pallas_call(
         functools.partial(kernel, sizes),
         out_shape=jax.ShapeDtypeStruct(sources.shape, f32),
-        in_specs=[pl.BlockSpec(memory_space=pltpu.VMEM)] * 5,
+        in_specs=[pl.BlockSpec(memory_space=pltpu.VMEM)] * 7,
         out_specs=pl.BlockSpec(memory_space=pltpu.VMEM),
         scratch_shapes=[
-            pltpu.VMEM((2, 2 * part, width), jnp.bfloat16),
+            pltpu.VMEM((2, width, 2 * part), jnp.bfloat16),
             pltpu.VMEM((items, part, width), f32),
             pltpu.VMEM((steps - 1, rows, width), f32),
-            pltpu.VMEM((items, far, blocks, part, order), f32),
-            pltpu.VMEM((items, far, blocks, part, order), f32),
+            pltpu.VMEM((items, far, blocks, order, part), f32),
+            pltpu.VMEM((items, far, blocks, order, part), f32),
             pltpu.VMEM(cells, f32),
             pltpu.VMEM(cells, f32),
             pltpu.VMEM(cells, f32),
@@ -274,9 +272,9 @@
             collective_id=0, has_side_effects=True, vmem_limit_bytes=60 * 2**20
         ),
         cost_estimate=pl.CostEstimate(
-            flops=6 * steps * rows * out_rows * tiles.shape[1], bytes_accessed=24 * 2**20, transcendentals=0
+            flops=6 * steps * rows * out_rows * 2 * width, bytes_accessed=24 * 2**20, transcendentals=0
         ),
-    )(m_high, m_low, history[0], sources, self_inverse)
+    )(*highs, *lows, history[0], sources, self_inverse)
 
 
 def solution(mesh):

time: 397 us -> 409 us (1.030)
  local copies, waits for them, and re-layouts: 15.8 us -> 23.9 us
  other arithmetic: 6.98 us -> 12.6 us
    slice x0 -> x1, local copies, waits for them, and re-layouts: none -> 19.2 us  [on_device(): halves = [delays[0, :, h, :] for h in range(2)]]
    unnamed x2 -> x1, local copies, waits for them, and re-layouts: 15.8 us -> 4.79 us
    convert_element_type x1, other arithmetic: 6.98 us -> 12.6 us  [on_device(): lows = [(half - x).astype(jnp.bfloat16) for half, x in zip(halves, rounded)]]
where the time goes in v2:
time: 409 us
  Pallas kernels  373 us (91%)
  local copies, waits for them, and re-layouts  23.9 us (6%)
  other arithmetic  12.6 us (3%)
    pallas_call x1, Pallas kernels, on_device(): pl.pallas_call(functools.partial(kernel, sizes), out_shape=jax.ShapeDtype...  373 us
    slice x1, local copies, waits for them, and re-layouts, on_device(): halves = [delays[0, :, h, :] for h in range(2)]  19.2 us
    convert_element_type x1, other arithmetic, on_device(): lows = [(half - x).astype(jnp.bfloat16) for half, x in zip(halves, rounded)]  12.6 us

profile of v2, /device:TPU:28, one launch (start us, length us, event | category | flops | bytes accessed | tf_op | source)
XLA Modules:
  0.0 409.3 jit_solution(3741856471835591395)
XLA Ops:
  0.0 19.2 %fusion.2 = (f32[1,2048,1,1024]{3,2,1,0:T(1,128)S(1)}, f32[1,2048,1,1024]{3,2,1,0:T(1,128)}) fusion(f32[1,2048,2,1024]{3,2,1,0:T(2,128)} %param.4), kind=kLoop, calls=%fused_computation.8 | loop fusion | bytes 33554432 | tf_op jit(solution)/shard_map/slice | solution.py:232
  19.2 12.6 %fusion = (bf16[2048,1024]{1,0:T(8,128)(2,1)}, bf16[2048,1024]{1,0:T(8,128)(2,1)}, bf16[2048,1024]{1,0:T(8,128)(2,1)}, bf16[2048,1024]{1,0:T(8,128)(2,1)}) fusion(f32[1,2048,1,1024]{3,2,1,0:T(1,128)} %get-tuple-element.6, f32[1,2048,1,1024]{3,2,1,0:T(1,128)S(1)} %get-tuple-element.5), kind=kLoop, calls=%fused_computation.4 | loop fusion | flops 16777216 | bytes 33554432 | tf_op jit(solution)/shard_map/convert_element_type | solution.py:235
  31.7 372.8 %shard_map.46 = f32[4,256,1024]{2,1,0:T(8,128)} custom-call(bf16[2048,1024]{1,0:T(8,128)(2,1)} %get-tuple-element.10.high_0, bf16[2048,1024]{1,0:T(8,128)(2,1)} %get-tuple-element.11.high_1, bf16[2048,1024]{1,0:T(8,128)(2,1)} %get-tuple-element.9.low_0, bf16[2048,1024]{1,0:T(8,128)(2,1)} %get-tuple-element.12.low_1, f32[256,1024]{1,0:T(8,128)} %bitcast.13, ...), custom_call_target="tpu_custom_call" | custom-call | flops 25769803776 | bytes 25165824 | tf_op jit(solution)/shard_map/pallas_call | solution.py:244
  404.5 4.8 %copy.20 = f32[4,256,1024]{2,1,0:T(8,128)} copy(f32[4,256,1024]{2,1,0:T(8,128)} %shard_map.46) | data formatting | bytes 8388608

commit v3 on v2

--- a/solution.py
+++ b/solution.py
@@ -22,7 +22,7 @@
 
 
 def kernel(
-    sizes, high_0, high_1, low_0, low_1, hist, sources, inverse, out,
+    sizes, m_high, m_low, hist, sources, inverse, out,
     xs, partner, older, p_send, p_recv, total, z_recv, y_recv,
     x_send_sem, x_recv_sem, z_send_sem, z_recv_sem, y_recv_sem,
     b_one_sem, b_two_sem, b_recv_sem, r_send_sem, r_recv_sem, h_send_sem, h_recv_sem,
@@ -86,9 +86,10 @@
     def tile(first):
         at = pl.ds(pl.multiple_of(first, order), order)
         acc = jnp.zeros((order, part), jnp.float32)
-        for h, (m_high, m_low) in enumerate(((high_0, low_0), (high_1, low_1))):
-            both = times(m_high[at], xs[h])
-            acc = acc + (both[:, :part] + both[:, part:] + times(m_low[at], xs[h, :, :part]))
+        for h in range(2):
+            here = slice(h * width, (h + 1) * width)
+            both = times(m_high[at, here], xs[h])
+            acc = acc + (both[:, :part] + both[:, part:] + times(m_low[at, here], xs[h, :, :part]))
         return acc
 
     def p_copy(n, by, b):
@@ -199,13 +200,17 @@
         def _():
             lax.fori_loop(0, blocks, one, 0)
 
+    last = items + GROUPS
+    lag = jnp.where(k < steps - 1, 2 * GROUPS, last)
+
     def turn(i, carry):
         pl.when((i >= GROUPS) & (i < items + GROUPS))(lambda: reduce(i - GROUPS))
-        pl.when(i >= 2 * GROUPS)(lambda: pass_on(i - 2 * GROUPS))
+        late = i - lag
+        pl.when((late >= 0) & (late < items))(lambda: pass_on(late))
         pl.when(i < items)(lambda: multiply(i))
         return carry
 
-    lax.fori_loop(0, items + 2 * GROUPS, turn, 0)
+    lax.fori_loop(0, items + last, turn, 0)
 
     def whole_send(ref, sem):
         remote(ref, ref, sem, sem, row=1 - r).wait_send()
@@ -229,10 +234,10 @@
 
 def on_device(n_delay, n_col, delays, history, sources, self_inverse):
     out_rows = delays.shape[1]
-    halves = [delays[0, :, h, :] for h in range(2)]
-    rounded = [lax.reduce_precision(half, 8, 7) for half in halves]
-    highs = [x.astype(jnp.bfloat16) for x in rounded]
-    lows = [(half - x).astype(jnp.bfloat16) for half, x in zip(halves, rounded)]
+    tiles = delays.reshape(out_rows, -1)
+    rounded = lax.reduce_precision(tiles, 8, 7)
+    m_high = rounded.astype(jnp.bfloat16)
+    m_low = (tiles - rounded).astype(jnp.bfloat16)
     steps, rows, width = sources.shape
     blocks, order, _ = self_inverse.shape
     items, part = steps * GROUPS, rows // GROUPS
@@ -244,7 +249,7 @@
     return pl.pallas_call(
         functools.partial(kernel, sizes),
         out_shape=jax.ShapeDtypeStruct(sources.shape, f32),
-        in_specs=[pl.BlockSpec(memory_space=pltpu.VMEM)] * 7,
+        in_specs=[pl.BlockSpec(memory_space=pltpu.VMEM)] * 5,
         out_specs=pl.BlockSpec(memory_space=pltpu.VMEM),
         scratch_shapes=[
             pltpu.VMEM((2, width, 2 * part), jnp.bfloat16),
@@ -274,7 +279,7 @@
         cost_estimate=pl.CostEstimate(
             flops=6 * steps * rows * out_rows * 2 * width, bytes_accessed=24 * 2**20, transcendentals=0
         ),
-    )(*highs, *lows, history[0], sources, self_inverse)
+    )(m_high, m_low, history[0], sources, self_inverse)
 
 
 def solution(mesh):

time: 409 us -> 248 us (0.61)
  Pallas kernels: 373 us -> 225 us
  local copies, waits for them, and re-layouts: 23.9 us -> 15.8 us
  other arithmetic: 12.6 us -> 6.98 us
    pallas_call x1, Pallas kernels: 373 us -> 225 us  [on_device(): pl.pallas_call(functools.partial(kernel, sizes), out_shape=jax.ShapeDtype...]
    slice x1 -> x0, local copies, waits for them, and re-layouts: 19.2 us -> none  [on_device(): halves = [delays[0, :, h, :] for h in range(2)]]
    unnamed x1 -> x2, local copies, waits for them, and re-layouts: 4.79 us -> 15.8 us
    convert_element_type x1, other arithmetic: 12.6 us -> 6.98 us  [on_device(): m_low = (tiles - rounded).astype(jnp.bfloat16)]
where the time goes in v3:
time: 248 us
  Pallas kernels  225 us (91%)
  local copies, waits for them, and re-layouts  15.8 us (6%)
  other arithmetic  6.98 us (3%)
    pallas_call x1, Pallas kernels, on_device(): pl.pallas_call(functools.partial(kernel, sizes), out_shape=jax.ShapeDtype...  225 us
    unnamed x2, local copies, waits for them, and re-layouts  15.8 us
    convert_element_type x1, other arithmetic, on_device(): m_low = (tiles - rounded).astype(jnp.bfloat16)  6.98 us

profile of v3, /device:TPU:28, one launch (start us, length us, event | category | flops | bytes accessed | tf_op | source)
XLA Modules:
  0.0 248.3 jit_solution(805437825536621008)
XLA Ops:
  0.0 11.0 %copy.5 = f32[256,8,2,1024]{3,1,2,0:T(8,128)S(1)} copy(f32[256,8,2,1024]{3,2,1,0:T(2,128)} %bitcast.5) | data formatting | bytes 33554432
  11.0 7.0 %fusion = (bf16[2048,2048]{1,0:T(8,128)(2,1)}, bf16[2048,2048]{1,0:T(8,128)(2,1)}) fusion(f32[2048,2048]{1,0:T(8,128)S(1)} %bitcast.4), kind=kLoop, calls=%fused_computation.2 | loop fusion | flops 16777216 | bytes 33554432 | tf_op jit(solution)/shard_map/convert_element_type | solution.py:240
  18.0 225.4 %shard_map.46 = f32[4,256,1024]{2,1,0:T(8,128)} custom-call(bf16[2048,2048]{1,0:T(8,128)(2,1)} %get-tuple-element.6.m_high, bf16[2048,2048]{1,0:T(8,128)(2,1)} %get-tuple-element.5.m_low, f32[256,1024]{1,0:T(8,128)} %bitcast.6, f32[4,256,1024]{2,1,0:T(8,128)} %sources.1, f32[4,256,256]{2,1,0:T(8,128)} %inverse.1), custom_call_target="tpu_custom_call" | custom-call | flops 25769803776 | bytes 25165824 | tf_op jit(solution)/shard_map/pallas_call | solution.py:249
  243.5 4.8 %copy.7 = f32[4,256,1024]{2,1,0:T(8,128)} copy(f32[4,256,1024]{2,1,0:T(8,128)} %shard_map.46) | data formatting | bytes 8388608

commit v4 on v3

--- a/solution.py
+++ b/solution.py
@@ -36,6 +36,7 @@
     c = lax.axis_index("col")
     has_one = k + 1 < n_delay
     has_two = k + 2 < n_delay
+    even = k % 2 == 0
 
     def remote(src, dst, send, recv, **where):
         return pltpu.make_async_remote_copy(
@@ -193,7 +194,8 @@
 
         def one(b, carry):
             arrived(cell(s, g, b), b_recv_sem.at[n, b])
-            pl.when(has_two)(lambda: b_copy(n, b, 2, b_two_sem).start())
+            pl.when(has_two & even)(lambda: b_copy(n, b, 2, b_two_sem).start())
+            pl.when(has_one & even)(lambda: b_copy(n, b, 1, b_one_sem).start())
             return carry
 
         @pl.when(k >= 1)
@@ -201,7 +203,7 @@
             lax.fori_loop(0, blocks, one, 0)
 
     last = items + GROUPS
-    lag = jnp.where(k < steps - 1, 2 * GROUPS, last)
+    lag = jnp.where(k == 0, last, jnp.where(k == 1, 4, jnp.where(k == 2, 5, jnp.where(even, 6, last))))
 
     def turn(i, carry):
         pl.when((i >= GROUPS) & (i < items + GROUPS))(lambda: reduce(i - GROUPS))
@@ -221,8 +223,8 @@
             whole_send(p_send.at[n, by - 1], x_send_sem.at[n, by - 1])
         whole_send(partner.at[n], r_send_sem.at[n])
         pl.when(k >= 1)(lambda: whole_send(total.at[n], z_send_sem.at[n]))
-        pl.when(k == 0)(lambda: whole_send(out.at[s, rows_of(g)], b_one_sem.at[n]))
-        pl.when(has_two)(lambda: whole_send(out.at[s, rows_of(g)], b_two_sem.at[n]))
+        pl.when(has_one & even)(lambda: whole_send(out.at[s, rows_of(g)], b_one_sem.at[n]))
+        pl.when(has_two & even)(lambda: whole_send(out.at[s, rows_of(g)], b_two_sem.at[n]))
         return carry
 
     lax.fori_loop(0, items, settle, 0)

time: 248 us -> 269 us (1.085)
  Pallas kernels: 225 us -> 246 us
    pallas_call x1, Pallas kernels: 225 us -> 246 us  [on_device(): pl.pallas_call(functools.partial(kernel, sizes), out_shape=jax.ShapeDtype...]
where the time goes in v4:
time: 269 us
  Pallas kernels  246 us (91%)
  local copies, waits for them, and re-layouts  15.8 us (6%)
  other arithmetic  6.98 us (3%)
    pallas_call x1, Pallas kernels, on_device(): pl.pallas_call(functools.partial(kernel, sizes), out_shape=jax.ShapeDtype...  246 us
    unnamed x2, local copies, waits for them, and re-layouts  15.8 us
    convert_element_type x1, other arithmetic, on_device(): m_low = (tiles - rounded).astype(jnp.bfloat16)  6.98 us

profile of v4, /device:TPU:28, one launch (start us, length us, event | category | flops | bytes accessed | tf_op | source)
XLA Modules:
  0.0 268.6 jit_solution(12865810315828499687)
XLA Ops:
  0.0 11.0 %copy.5 = f32[256,8,2,1024]{3,1,2,0:T(8,128)S(1)} copy(f32[256,8,2,1024]{3,2,1,0:T(2,128)} %bitcast.5) | data formatting | bytes 33554432
  11.0 7.0 %fusion = (bf16[2048,2048]{1,0:T(8,128)(2,1)}, bf16[2048,2048]{1,0:T(8,128)(2,1)}) fusion(f32[2048,2048]{1,0:T(8,128)S(1)} %bitcast.4), kind=kLoop, calls=%fused_computation.2 | loop fusion | flops 16777216 | bytes 33554432 | tf_op jit(solution)/shard_map/convert_element_type | solution.py:242
  18.0 245.8 %shard_map.46 = f32[4,256,1024]{2,1,0:T(8,128)} custom-call(bf16[2048,2048]{1,0:T(8,128)(2,1)} %get-tuple-element.6.m_high, bf16[2048,2048]{1,0:T(8,128)(2,1)} %get-tuple-element.5.m_low, f32[256,1024]{1,0:T(8,128)} %bitcast.6, f32[4,256,1024]{2,1,0:T(8,128)} %sources.1, f32[4,256,256]{2,1,0:T(8,128)} %inverse.1), custom_call_target="tpu_custom_call" | custom-call | flops 25769803776 | bytes 25165824 | tf_op jit(solution)/shard_map/pallas_call | solution.py:251
  263.9 4.8 %copy.7 = f32[4,256,1024]{2,1,0:T(8,128)} copy(f32[4,256,1024]{2,1,0:T(8,128)} %shard_map.46) | data formatting | bytes 8388608

commit v5 on v3

--- a/solution.py
+++ b/solution.py
@@ -36,6 +36,10 @@
     c = lax.axis_index("col")
     has_one = k + 1 < n_delay
     has_two = k + 2 < n_delay
+    can_pair = n_col == 2 and blocks % 2 == 0 and n_delay % 2 == 0
+    paired = (k >= 2) if can_pair else False
+    mate = 1 - 2 * (k % 2)
+    half = blocks // 2
 
     def remote(src, dst, send, recv, **where):
         return pltpu.make_async_remote_copy(
@@ -98,6 +102,21 @@
             x_send_sem.at[n, by - 1], x_recv_sem.at[n, by - 1, b], col=col_at(by),
         )
 
+    def mate_copy(n, b):
+        return remote(
+            p_send.at[n, 0, b], y_recv.at[n, b], x_send_sem.at[n, 0], y_recv_sem.at[n, b], delay=k + mate,
+        )
+
+    def merge(n):
+        def one(i, carry):
+            b = i + (k % 2) * half
+            arrived(y_recv.at[n, b], y_recv_sem.at[n, b])
+            p_send[n, 0, b] = p_send[n, 0, b] + y_recv[n, b]
+            p_copy(n, 1, b).start()
+            return carry
+
+        lax.fori_loop(0, half, one, 0)
+
     def multiply(n):
         s, g = n // GROUPS, n % GROUPS
 
@@ -126,9 +145,14 @@
         put(1 - r, partner[n])
 
         for by in range(1, n_col):
-            def far(b, carry):
+            def far(i, carry):
+                b = (i + (1 - k % 2) * half) % blocks if can_pair else i
                 p_send[n, by - 1, b] = tile((col_at(by) * blocks + b) * order)
-                p_copy(n, by, b).start()
+                if can_pair:
+                    pl.when(jnp.logical_not(paired))(lambda: p_copy(n, by, b).start())
+                    pl.when(paired & (i < half))(lambda: mate_copy(n, b).start())
+                else:
+                    p_copy(n, by, b).start()
                 return carry
 
             lax.fori_loop(0, blocks, far, 0)
@@ -157,11 +181,17 @@
         s, g = n // GROUPS, n % GROUPS
 
         def one(b, carry):
-            value = total[n, b]
-            for by in range(1, n_col):
-                arrived(p_recv.at[n, by - 1, b], x_recv_sem.at[n, by - 1, b])
-                value = value + p_recv[n, by - 1, b]
-            total[n, b] = value
+            def take():
+                value = total[n, b]
+                for by in range(1, n_col):
+                    arrived(p_recv.at[n, by - 1, b], x_recv_sem.at[n, by - 1, b])
+                    value = value + p_recv[n, by - 1, b]
+                total[n, b] = value
+
+            if can_pair:
+                pl.when(jnp.logical_not(paired) | (b // half == k % 2))(take)
+            else:
+                take()
 
             @pl.when(has_two)
             def _():
@@ -200,17 +230,18 @@
         def _():
             lax.fori_loop(0, blocks, one, 0)
 
-    last = items + GROUPS
-    lag = jnp.where(k < steps - 1, 2 * GROUPS, last)
+    lag = jnp.where(k < 2, 2 * GROUPS, jnp.where(k < steps - 1, 3 * GROUPS, items))
 
     def turn(i, carry):
+        if can_pair:
+            pl.when(paired & (i >= 1) & (i <= items))(lambda: merge(i - 1))
         pl.when((i >= GROUPS) & (i < items + GROUPS))(lambda: reduce(i - GROUPS))
         late = i - lag
         pl.when((late >= 0) & (late < items))(lambda: pass_on(late))
         pl.when(i < items)(lambda: multiply(i))
         return carry
 
-    lax.fori_loop(0, items + last, turn, 0)
+    lax.fori_loop(0, 2 * items, turn, 0)
 
     def whole_send(ref, sem):
         remote(ref, ref, sem, sem, row=1 - r).wait_send()

time: 248 us -> 281 us (1.13)
  Pallas kernels: 225 us -> 258 us
    pallas_call x1, Pallas kernels: 225 us -> 258 us  [on_device(): pl.pallas_call(functools.partial(kernel, sizes), out_shape=jax.ShapeDtype...]
where the time goes in v5:
time: 281 us; the launch traced here: 280 us
  Pallas kernels  258 us (92%)
  local copies, waits for them, and re-layouts  15.8 us (6%)
  other arithmetic  6.98 us (2%)
    pallas_call x1, Pallas kernels, on_device(): pl.pallas_call(functools.partial(kernel, sizes), out_shape=jax.ShapeDtype...  258 us
    unnamed x2, local copies, waits for them, and re-layouts  15.8 us
    convert_element_type x1, other arithmetic, on_device(): m_low = (tiles - rounded).astype(jnp.bfloat16)  6.98 us

profile of v5, /device:TPU:28, one launch (start us, length us, event | category | flops | bytes accessed | tf_op | source)
XLA Modules:
  0.0 280.4 jit_solution(7209167081378501719)
XLA Ops:
  0.0 11.0 %copy.5 = f32[256,8,2,1024]{3,1,2,0:T(8,128)S(1)} copy(f32[256,8,2,1024]{3,2,1,0:T(2,128)} %bitcast.5) | data formatting | bytes 33554432
  11.0 7.0 %fusion = (bf16[2048,2048]{1,0:T(8,128)(2,1)}, bf16[2048,2048]{1,0:T(8,128)(2,1)}) fusion(f32[2048,2048]{1,0:T(8,128)S(1)} %bitcast.4), kind=kLoop, calls=%fused_computation.2 | loop fusion | flops 16777216 | bytes 33554432 | tf_op jit(solution)/shard_map/convert_element_type | solution.py:271
  18.0 257.6 %shard_map.46 = f32[4,256,1024]{2,1,0:T(8,128)} custom-call(bf16[2048,2048]{1,0:T(8,128)(2,1)} %get-tuple-element.6.m_high, bf16[2048,2048]{1,0:T(8,128)(2,1)} %get-tuple-element.5.m_low, f32[256,1024]{1,0:T(8,128)} %bitcast.6, f32[4,256,1024]{2,1,0:T(8,128)} %sources.1, f32[4,256,256]{2,1,0:T(8,128)} %inverse.1), custom_call_target="tpu_custom_call" | custom-call | flops 25769803776 | bytes 25165824 | tf_op jit(solution)/shard_map/pallas_call | solution.py:280
  275.6 4.8 %copy.7 = f32[4,256,1024]{2,1,0:T(8,128)} copy(f32[4,256,1024]{2,1,0:T(8,128)} %shard_map.46) | data formatting | bytes 8388608

commit v6 on v3

--- a/solution.py
+++ b/solution.py
@@ -36,6 +36,10 @@
     c = lax.axis_index("col")
     has_one = k + 1 < n_delay
     has_two = k + 2 < n_delay
+    has_four = k + 4 < n_delay
+    middle = (k == 2) | (k == 3)
+    above = (k == 4) | (k == 5)
+    early = items // 2
 
     def remote(src, dst, send, recv, **where):
         return pltpu.make_async_remote_copy(
@@ -61,8 +65,10 @@
     pl.when(has_two)(lambda: greet(delay=k + 2))
     pl.when(k >= 1)(lambda: greet(delay=k - 1))
     pl.when(k >= 2)(lambda: greet(delay=k - 2))
+    pl.when(has_four)(lambda: greet(delay=k + 4))
+    pl.when(k >= 4)(lambda: greet(delay=k - 4))
     peers = n_col
-    for there in (has_one, has_two, k >= 1, k >= 2):
+    for there in (has_one, has_two, has_four, k >= 1, k >= 2, k >= 4):
         peers = peers + jnp.where(there, 1, 0)
     pl.semaphore_wait(barrier, peers)
 
@@ -193,7 +199,8 @@
 
         def one(b, carry):
             arrived(cell(s, g, b), b_recv_sem.at[n, b])
-            pl.when(has_two)(lambda: b_copy(n, b, 2, b_two_sem).start())
+            pl.when(has_two & ~(above & (n < early)))(lambda: b_copy(n, b, 2, b_two_sem).start())
+            pl.when(has_four & middle & (n < early))(lambda: b_copy(n, b, 4, b_one_sem).start())
             return carry
 
         @pl.when(k >= 1)
@@ -201,7 +208,7 @@
             lax.fori_loop(0, blocks, one, 0)
 
     last = items + GROUPS
-    lag = jnp.where(k < steps - 1, 2 * GROUPS, last)
+    lag = jnp.where(k < 3, 2 * GROUPS, jnp.where(k == 3, 3 * GROUPS, last))
 
     def turn(i, carry):
         pl.when((i >= GROUPS) & (i < items + GROUPS))(lambda: reduce(i - GROUPS))
@@ -221,8 +228,10 @@
             whole_send(p_send.at[n, by - 1], x_send_sem.at[n, by - 1])
         whole_send(partner.at[n], r_send_sem.at[n])
         pl.when(k >= 1)(lambda: whole_send(total.at[n], z_send_sem.at[n]))
-        pl.when(k == 0)(lambda: whole_send(out.at[s, rows_of(g)], b_one_sem.at[n]))
-        pl.when(has_two)(lambda: whole_send(out.at[s, rows_of(g)], b_two_sem.at[n]))
+        one_used = (k == 0) | (has_four & middle & (n < early))
+        pl.when(one_used)(lambda: whole_send(out.at[s, rows_of(g)], b_one_sem.at[n]))
+        two_used = has_two & ~(above & (n < early))
+        pl.when(two_used)(lambda: whole_send(out.at[s, rows_of(g)], b_two_sem.at[n]))
         return carry
 
     lax.fori_loop(0, items, settle, 0)

time: 248 us -> 260 us (1.048)
  Pallas kernels: 225 us -> 237 us
    pallas_call x1, Pallas kernels: 225 us -> 237 us  [on_device(): pl.pallas_call(functools.partial(kernel, sizes), out_shape=jax.ShapeDtype...]
where the time goes in v6:
time: 260 us
  Pallas kernels  237 us (91%)
  local copies, waits for them, and re-layouts  15.8 us (6%)
  other arithmetic  6.98 us (3%)
    pallas_call x1, Pallas kernels, on_device(): pl.pallas_call(functools.partial(kernel, sizes), out_shape=jax.ShapeDtype...  237 us
    unnamed x2, local copies, waits for them, and re-layouts  15.8 us
    convert_element_type x1, other arithmetic, on_device(): m_low = (tiles - rounded).astype(jnp.bfloat16)  6.98 us

profile of v6, /device:TPU:28, one launch (start us, length us, event | category | flops | bytes accessed | tf_op | source)
XLA Modules:
  0.0 259.6 jit_solution(14529830342732095555)
XLA Ops:
  0.0 11.0 %copy.5 = f32[256,8,2,1024]{3,1,2,0:T(8,128)S(1)} copy(f32[256,8,2,1024]{3,2,1,0:T(2,128)} %bitcast.5) | data formatting | bytes 33554432
  11.0 7.0 %fusion = (bf16[2048,2048]{1,0:T(8,128)(2,1)}, bf16[2048,2048]{1,0:T(8,128)(2,1)}) fusion(f32[2048,2048]{1,0:T(8,128)S(1)} %bitcast.4), kind=kLoop, calls=%fused_computation.2 | loop fusion | flops 16777216 | bytes 33554432 | tf_op jit(solution)/shard_map/convert_element_type | solution.py:249
  18.0 236.8 %shard_map.46 = f32[4,256,1024]{2,1,0:T(8,128)} custom-call(bf16[2048,2048]{1,0:T(8,128)(2,1)} %get-tuple-element.6.m_high, bf16[2048,2048]{1,0:T(8,128)(2,1)} %get-tuple-element.5.m_low, f32[256,1024]{1,0:T(8,128)} %bitcast.6, f32[4,256,1024]{2,1,0:T(8,128)} %sources.1, f32[4,256,256]{2,1,0:T(8,128)} %inverse.1), custom_call_target="tpu_custom_call" | custom-call | flops 25769803776 | bytes 25165824 | tf_op jit(solution)/shard_map/pallas_call | solution.py:258
  254.8 4.8 %copy.7 = f32[4,256,1024]{2,1,0:T(8,128)} copy(f32[4,256,1024]{2,1,0:T(8,128)} %shard_map.46) | data formatting | bytes 8388608
